TPU v7x, 128 devices: a whole 4x4x4 slice. The times are simulated.
128 devices in a mesh: resp: 16 (over z, x_hi, core), ctx: 8 (over y, x_lo).
Axes of the slice: x: 4 (x_hi: 2, x_lo: 2; x = x_hi * 2 + x_lo), y: 4, z: 4, core: 2. Of those that a mesh axis runs over, the one named last changes fastest.
Arguments:
- queries: bfloat16 [16, 1024, 8192], P('resp', 'ctx'), may hold values from -5 to 5
- resp_keys: bfloat16 [16, 1024, 1024], P('resp', 'ctx'), may hold values from -5 to 5
- resp_values: bfloat16 [16, 1024, 1024], P('resp', 'ctx'), may hold values from -6 to 6
- prompt_keys: bfloat16 [256, 1024], P(('resp', 'ctx')), may hold values from -5 to 5
- prompt_values: bfloat16 [256, 1024], P(('resp', 'ctx')), may hold values from -6 to 6
- upstream: bfloat16 [16, 1024, 8192], P('resp', 'ctx'), may hold values from -6 to 6
- lengths: int32 [16], P('resp'), may hold values from 256 to 1024, as said below
- prompt_length: int32 [1], replicated, may hold values from 64 to 256
Outputs:
- attended: bfloat16 [16, 1024, 8192], P('resp', 'ctx')
- query_grads: bfloat16 [16, 1024, 8192], P('resp', 'ctx')
- key_grads: float32 [16, 1024, 1024], P('resp', 'ctx')
- value_grads: float32 [16, 1024, 1024], P('resp', 'ctx')
- prompt_keygrad: float32 [256, 1024], P(('resp', 'ctx'))
- prompt_valuegrad: float32 [256, 1024], P(('resp', 'ctx'))
Inputs may be any that keep to these rules, and one draw needn't show every extreme that they name: `lengths`: one response is live over all 1024 positions and one over exactly 256.
All inputs are finite; a program needn't handle non-finite values.
Results may differ from a plain program's by a relative error of at most 0.025.
Values may be sent and summed in bfloat16 or wider, within the bound.
A program may use at most 128 MiB of HBM per device.

v0:
```python
import jax
import jax.numpy as jnp
from jax import lax
from jax.sharding import PartitionSpec as P

H = 64
KVH = 8
HD = 128
G = 8


def per_device(
    queries, resp_keys, resp_values, prompt_keys, prompt_values, upstream, lengths, prompt_length
):
    all_pkeys, all_pvalues = (
        lax.all_gather(prompt_keys, ("resp", "ctx"), axis=0, tiled=True),
        lax.all_gather(prompt_values, ("resp", "ctx"), axis=0, tiled=True),
    )
    tokens = queries.shape[1]
    my_block = lax.axis_index("ctx")
    cycle_keys, cycle_values = (
        lax.all_gather(resp_keys[0], "ctx", axis=0, tiled=True),
        lax.all_gather(resp_values[0], "ctx", axis=0, tiled=True),
    )
    prompt_rows = all_pkeys.shape[0]
    key_rows = prompt_rows + cycle_keys.shape[0]
    key_block = jnp.concatenate([all_pkeys, cycle_keys], 0)
    value_block = jnp.concatenate([all_pvalues, cycle_values], 0)
    position = my_block * tokens + jnp.arange(tokens, dtype=jnp.int32)
    live = position < lengths[0]
    key_index = jnp.arange(key_rows, dtype=jnp.int32)
    visible = ((key_index < prompt_rows) & (key_index < prompt_length[0]))[None, :] | (
        key_index >= prompt_rows
    )[None, :] & (key_index[None, :] - prompt_rows <= position[:, None])
    scaling = HD ** (-0.5)
    width = G * HD
    query_rows = queries[0]
    grad_rows = jnp.where(live[:, None], upstream[0], jnp.zeros((), upstream.dtype))

    def one_group(group_index, carry):
        attended, query_grads, key_terms, value_terms = carry
        qgroup = lax.dynamic_slice_in_dim(query_rows, group_index * width, width, 1).reshape(
            tokens, G, HD
        )
        ggroup = lax.dynamic_slice_in_dim(grad_rows, group_index * width, width, 1).reshape(
            tokens, G, HD
        )
        kgroup = lax.dynamic_slice_in_dim(key_block, group_index * HD, HD, 1)
        vgroup = lax.dynamic_slice_in_dim(value_block, group_index * HD, HD, 1)
        scores = (
            jnp.einsum("tjd,kd->tjk", qgroup, kgroup, preferred_element_type=jnp.float32) * scaling
        )
        scores = jnp.where(visible[:, None, :], scores, -jnp.inf)
        top = jnp.max(scores, axis=-1, keepdims=True)
        expo = jnp.exp(scores - top)
        weights = expo / jnp.sum(expo, axis=-1, keepdims=True)
        weights_low = weights.astype(jnp.bfloat16)
        mixed = jnp.einsum("tjk,kd->tjd", weights_low, vgroup, preferred_element_type=jnp.float32)
        result = jnp.where(live[:, None, None], mixed, 0.0).astype(jnp.bfloat16)
        correction = jnp.sum(ggroup.astype(jnp.float32) * result.astype(jnp.float32), axis=-1)
        prob_grad = jnp.einsum("tjd,kd->tjk", ggroup, vgroup, preferred_element_type=jnp.float32)
        score_grad = (weights * (prob_grad - correction[..., None]) * scaling).astype(jnp.bfloat16)
        qgrad = jnp.einsum(
            "tjk,kd->tjd", score_grad, kgroup, preferred_element_type=jnp.float32
        ).astype(jnp.bfloat16)
        key_term = jnp.einsum("tjk,tjd->kd", score_grad, qgroup, preferred_element_type=jnp.float32)
        value_term = jnp.einsum(
            "tjk,tjd->kd", weights_low, ggroup, preferred_element_type=jnp.float32
        )
        attended = lax.dynamic_update_slice_in_dim(
            attended, result.reshape(tokens, width), group_index * width, 1
        )
        query_grads = lax.dynamic_update_slice_in_dim(
            query_grads, qgrad.reshape(tokens, width), group_index * width, 1
        )
        key_terms = lax.dynamic_update_slice_in_dim(key_terms, key_term, group_index * HD, 1)
        value_terms = lax.dynamic_update_slice_in_dim(value_terms, value_term, group_index * HD, 1)
        return (attended, query_grads, key_terms, value_terms)

    start = (
        jnp.zeros((tokens, H * HD), jnp.bfloat16),
        jnp.zeros((tokens, H * HD), jnp.bfloat16),
        jnp.zeros((key_rows, KVH * HD), jnp.float32),
        jnp.zeros((key_rows, KVH * HD), jnp.float32),
    )
    attended, query_grads, key_terms, value_terms = lax.fori_loop(0, KVH, one_group, start)
    key_grads, value_grads = (
        lax.psum_scatter(
            key_terms[prompt_rows:].astype(jnp.bfloat16), "ctx", scatter_dimension=0, tiled=True
        ).astype(jnp.float32),
        lax.psum_scatter(
            value_terms[prompt_rows:].astype(jnp.bfloat16), "ctx", scatter_dimension=0, tiled=True
        ).astype(jnp.float32),
    )
    prompt_keygrad, prompt_valuegrad = (
        lax.psum_scatter(key_terms[:prompt_rows], ("resp", "ctx"), scatter_dimension=0, tiled=True),
        lax.psum_scatter(
            value_terms[:prompt_rows], ("resp", "ctx"), scatter_dimension=0, tiled=True
        ),
    )
    return (
        attended[None],
        query_grads[None],
        key_grads[None],
        value_grads[None],
        prompt_keygrad,
        prompt_valuegrad,
    )


def solution(mesh):
    placed = (
        P("resp", "ctx", None),
        P("resp", "ctx", None),
        P("resp", "ctx", None),
        P(("resp", "ctx"), None),
        P(("resp", "ctx"), None),
        P("resp", "ctx", None),
        P("resp"),
        P(),
    )
    return jax.shard_map(
        per_device,
        mesh=mesh,
        in_specs=placed,
        out_specs=(
            P("resp", "ctx", None),
            P("resp", "ctx", None),
            P("resp", "ctx", None),
            P("resp", "ctx", None),
            P(("resp", "ctx"), None),
            P(("resp", "ctx"), None),
        ),
        check_vma=False,
    )
```

profile of v0, /device:TPU:0, one launch (start us, length us, event | category | flops | bytes accessed | tf_op | source)
XLA Modules:
  0.0 1128.1 jit_solution(7431690782607835182)
XLA Ops:
  10.5 3.2 copy.50
  14.4 321.2 %all-gather.3 = bf16[128,2,1024]{2,1,0:T(2,128)(2,1)S(1)} all-gather(bf16[1,2,1024]{2,1,0:T(2,128)(2,1)S(1)} %bitcast.110), channel_id=1, replica_groups=mesh['resp'=16,'ctx'=8] {'resp','ctx'}, dimensions={0}, use_global_device_ids=true | all-gather | bytes 528384 | tf_op jit(solution)/shard_map/all_gather | solution.py:17
  336.0 332.6 %all-gather.2 = bf16[128,2,1024]{2,1,0:T(2,128)(2,1)} all-gather(bf16[1,2,1024]{2,1,0:T(2,128)(2,1)S(1)} %bitcast.111), channel_id=1, replica_groups=mesh['resp'=16,'ctx'=8] {'resp','ctx'}, dimensions={0}, use_global_device_ids=true | all-gather | bytes 528384 | tf_op jit(solution)/shard_map/all_gather | solution.py:16
  669.9 4.1 copy.47
  675.5 3.2 pad_maximum_fusion.1
  680.6 3.0 broadcast.53
  683.5 3.0 broadcast.53.clone
  689.6 172.1 %while.20 = (s32[]{:T(128)}, bf16[128,8192]{1,0:T(8,128)(2,1)}, bf16[128,8192]{1,0:T(8,128)(2,1)}, f32[1280,1024]{1,0:T(8,128)}, f32[1280,1024]{1,0:T(8,128)}, /...) while((s32[]{:T(128)}, bf16[128,8192]{1,0:T(8,128)(2,1)}, ...), condition=%wide.region_4.5_spmd.clone, body=%wide.region_0.4_spmd.clone.sunk | while | flops 2029093376 | bytes 55145068 | solution.py:86
  690.7 4.3 exponential_reduce_fusion.2
  695.0 3.9 fusion.72
  699.6 2.0 fusion.73
  704.4 2.7 multiply_convert_fusion.2
  712.3 4.3 exponential_reduce_fusion.2
  716.5 3.9 fusion.72
  721.1 2.0 fusion.73
  726.0 2.7 multiply_convert_fusion.2
  733.8 4.3 exponential_reduce_fusion.2
  738.0 3.9 fusion.72
  742.6 2.0 fusion.73
  747.5 2.7 multiply_convert_fusion.2
  755.3 4.3 exponential_reduce_fusion.2
  759.6 3.9 fusion.72
  764.1 2.0 fusion.73
  769.0 2.7 multiply_convert_fusion.2
  776.8 4.3 exponential_reduce_fusion.2
  781.0 3.9 fusion.72
  785.6 2.0 fusion.73
  790.5 2.7 multiply_convert_fusion.2
  798.3 4.3 exponential_reduce_fusion.2
  802.6 3.9 fusion.72
  807.1 2.0 fusion.73
  810.2 1.8 fusion.75
  812.0 2.7 multiply_convert_fusion.2
  819.8 4.3 exponential_reduce_fusion.2
  824.1 3.9 fusion.72
  828.6 2.0 fusion.73
  833.5 2.7 multiply_convert_fusion.2
  841.3 4.3 exponential_reduce_fusion.2
  845.6 3.9 fusion.72
  850.1 2.0 fusion.73
  855.0 2.7 multiply_convert_fusion.2
  861.7 2.3 slice.16
  864.0 2.3 slice.17
  866.4 3.9 slice.22
  870.3 3.9 slice.23
  874.2 138.5 %all-reduce.5.cloned.1.call-done = (f32[256,1024]{1,0:T(8,128)}, f32[256,1024]{1,0:T(8,128)}) async-done(((f32[256,1024]{1,0:T(8,128)}, f32[256,1024]{1,0:T(8,128)}), (f32[256,1024]{1,0:T(8,128)}, f32[256,1024]{1,0:T(8,128)})) %all-reduce.5.cloned.1.call-update) | async-done | bytes 2097168
  1015.5 50.3 %reduce-scatter.5.cloned.1.call-done = bf16[128,1024]{1,0:T(8,128)(2,1)} async-done(((bf16[1024,1024]{1,0:T(8,128)(2,1)}), bf16[128,1024]{1,0:T(8,128)(2,1)}) %reduce-scatter.5.cloned.1.call-update) | async-done | bytes 262160 | tf_op jit(solution)/shard_map/reduce_scatter | solution.py:91
  1067.6 52.2 %reduce-scatter.3.cloned.1.call-done = bf16[128,1024]{1,0:T(8,128)(2,1)} async-done(((bf16[1024,1024]{1,0:T(8,128)(2,1)}), bf16[128,1024]{1,0:T(8,128)(2,1)}) %reduce-scatter.3.cloned.1.call-update) | async-done | bytes 262160 | tf_op jit(solution)/shard_map/reduce_scatter | solution.py:88
  (151 shorter events, 83.9 us)
Async XLA Ops:
  7.2 7.2 copy-start
  7.2 668.3 %all-gather.9.cloned.1.call-start = ((), (), s32[]{:S(2)}) async-start(), calls=%async_computation.5 | async-start | bytes 2359296 | tf_op jit(solution)/shard_map/all_gather | solution.py:23
  9.0 669.7 %all-gather.7.cloned.1.call-start = ((), (), s32[]{:S(2)}) async-start(), calls=%async_computation.4 | async-start | bytes 2359296 | tf_op jit(solution)/shard_map/all_gather | solution.py:22
  9.8 1003.0 %all-reduce.5.cloned.1.call-start = ((), (), s32[]{:S(2)}) async-start(), calls=%async_computation.6 | async-start | bytes 4194304
  10.5 325.5 %copy-start.1 = (bf16[2,1024]{1,0:T(2,128)(2,1)S(1)}, bf16[2,1024]{1,0:T(2,128)(2,1)}, u32[]{:S(2)}) copy-start(bf16[2,1024]{1,0:T(2,128)(2,1)} %param.13) | copy-start | bytes 12292
  695.0 9.4 slice-start
  699.6 4.9 slice-start.1
  716.5 9.4 slice-start
  721.1 4.9 slice-start.1
  738.0 9.4 slice-start
  742.6 4.9 slice-start.1
  759.6 9.4 slice-start
  764.1 4.9 slice-start.1
  781.0 9.4 slice-start
  785.6 4.9 slice-start.1
  802.6 9.5 slice-start
  807.1 4.9 slice-start.1
  824.1 9.4 slice-start
  828.6 4.9 slice-start.1
  845.6 9.4 slice-start
  850.1 4.9 slice-start.1
  866.3 199.4 %reduce-scatter.5.cloned.1.call-start = ((), (), s32[]{:S(2)}) async-start(), calls=%async_computation.3 | async-start | bytes 2359296 | tf_op jit(solution)/shard_map/reduce_scatter | solution.py:91
  870.3 249.5 %reduce-scatter.3.cloned.1.call-start = ((), (), s32[]{:S(2)}) async-start(), calls=%async_computation.2 | async-start | bytes 2359296 | tf_op jit(solution)/shard_map/reduce_scatter | solution.py:88
Sparse Core Ops, SparseCore 0:
  10.2 55.0 all-gather.8
  66.9 53.8 all-gather.6
  866.5 146.2 all-reduce.4
  1015.0 50.7 reduce-scatter.4
  1068.0 51.6 reduce-scatter.2
where the time goes:
time: 1130 us
  blocking collectives  654 us (58%)
  waiting for transfers between devices  242 us (21%)
  matrix products  109 us (10%)
  other arithmetic  56.1 us (5%)
  local copies, waits for them, and re-layouts  51.6 us (5%)
  between operations  15.2 us (1%)
    all_gather x1, blocking collectives, per_device(): lax.all_gather(prompt_keys, ('resp', 'ctx'), axis=0, tiled=True)  333 us
    all_gather x1, blocking collectives, per_device(): lax.all_gather(prompt_values, ('resp', 'ctx'), axis=0, tiled=True)  321 us
    unnamed x6, waiting for transfers between devices  139 us
    reduce_scatter x1, waiting for transfers between devices, per_device(): lax.psum_scatter(key_terms[prompt_rows:].astype(jnp.bfloat16), 'ctx', sca...  52.2 us
    reduce_scatter x1, waiting for transfers between devices, per_device(): lax.psum_scatter(value_terms[prompt_rows:].astype(jnp.bfloat16), 'ctx', s...  50.3 us
    sub x8, matrix products, one_group(): expo = jnp.exp(scores - top)  34.3 us
    convert_element_type x8, other arithmetic, one_group(): weights_low = weights.astype(jnp.bfloat16)  30.8 us
  transfers between devices with their start and end apart: 5, of which 3 were waited for; matrix products, arithmetic and copies ran while one was open for 2% of the time, Pallas kernels for 0%

commit v1 on v0

v1 whole, which is shorter than its diff:
```python
import functools

import jax
import jax.numpy as jnp
from jax import lax
from jax.experimental import pallas as pl
from jax.experimental.pallas import tpu as pltpu
from jax.sharding import PartitionSpec as P

HD = 128
KVH = 8
G = 8
ROWS = G * HD
TOK = 128
SCALE = HD**-0.5
LOG2E = 1.4426950408889634
HIDE = -1e30
NT = (((1,), (1,)), ((), ()))
F32 = jnp.float32
BF = jnp.bfloat16
MESH = pl.DeviceIdType.MESH


def iota(shape, axis):
    return lax.broadcasted_iota(jnp.int32, shape, axis)


def dot(a, b):
    return jnp.dot(a, b, preferred_element_type=F32)


def dot_nt(a, b):
    return lax.dot_general(a, b, NT, preferred_element_type=F32)


def kernel(
    nr, nc,
    q_hbm, d_hbm, k_ref, v_ref, pk_ref, pv_ref, len_ref, plen_ref,
    out_hbm, dq_hbm, kg_ref, vg_ref, pkg_ref, pvg_ref,
    qv, dv, ov, dqv, kv, term, rterm, hidden_cols, ones_cols, causal_cols,
    pown, prep, pterm, psum, pback,
    in_sem, out_sem,
    a_send, a_recv, b_send, b_recv, g_send, g_recv,
    t_send, t_recv, p_send, p_recv, z_send, z_recv,
):
    prow = 2 * nc
    prompt = nr * prow
    key_rows = prompt + nc * TOK
    r = lax.axis_index("resp")
    c = lax.axis_index("ctx")

    load_q = pltpu.make_async_copy(q_hbm, qv, in_sem.at[0])
    load_d = pltpu.make_async_copy(d_hbm, dv, in_sem.at[1])
    load_q.start()
    load_d.start()

    barrier = pltpu.get_barrier_semaphore()

    def others(n, me, body):
        def step(i, carry):
            body(lax.rem(me + i, n))
            return carry

        lax.fori_loop(1, n, step, 0)

    others(nc, c, lambda p: pl.semaphore_signal(barrier, inc=1, device_id={"ctx": p}, device_id_type=MESH))
    others(nr, r, lambda p: pl.semaphore_signal(barrier, inc=1, device_id={"resp": p}, device_id_type=MESH))

    def block_rows(j):
        return pl.ds(pl.multiple_of(prompt + j * TOK, TOK), TOK)

    pown[c, 0] = pk_ref[...]
    pown[c, 1] = pv_ref[...]
    for g in range(KVH):
        kv[g, 0, block_rows(c), :] = k_ref[:, g * HD:(g + 1) * HD]
        kv[g, 1, block_rows(c), :] = v_ref[:, g * HD:(g + 1) * HD]

    pl.semaphore_wait(barrier, nc - 1 + nr - 1)

    def copy_a(slot, peer):
        return pltpu.make_async_remote_copy(
            src_ref=pown.at[slot], dst_ref=pown.at[slot],
            send_sem=a_send.at[peer], recv_sem=a_recv.at[slot],
            device_id={"ctx": peer}, device_id_type=MESH)

    others(nc, c, lambda p: copy_a(c, p).start())

    def copy_g(g, slot, peer):
        return pltpu.make_async_remote_copy(
            src_ref=kv.at[g, :, block_rows(slot), :], dst_ref=kv.at[g, :, block_rows(slot), :],
            send_sem=g_send.at[g, peer], recv_sem=g_recv.at[g, slot],
            device_id={"ctx": peer}, device_id_type=MESH)

    def loop(lo, hi, body):
        def step(i, carry):
            body(i)
            return carry

        lax.fori_loop(lo, hi, step, 0)

    loop(0, KVH, lambda g: loop(c + 1, nc, lambda p: copy_g(g, c, p).start()))

    def clear(j):
        def one(g):
            kv[g, 0, block_rows(j), :] = jnp.zeros((TOK, HD), BF)
            kv[g, 1, block_rows(j), :] = jnp.zeros((TOK, HD), BF)
        loop(0, KVH, one)

    loop(c + 1, nc, clear)

    row = iota((key_rows, HD), 0)
    col = iota((key_rows, HD), 1)
    gone = ((row < prompt) & (row >= plen_ref[0])) | (row >= prompt + (c + 1) * TOK)
    diagonal = (row - (prompt + c * TOK) == col) & (col > 0)
    hidden_cols[...] = jnp.where(diagonal, 1.0, jnp.where(gone & (col == 0), HIDE, 0.0)).astype(BF)
    ones_cols[...] = jnp.where(col < 2, 1.0, 0.0).astype(BF)
    tok = iota((TOK, HD), 0)
    key = iota((TOK, HD), 1)
    causal_cols[...] = jnp.where(key == 0, 1.0, jnp.where(key > tok, HIDE, 0.0)).astype(BF)
    live = c * TOK + tok < len_ref[0]
    live_lane = jnp.where(c * TOK + iota((1, TOK), 1) < len_ref[0], 1.0, 0.0)

    n16 = 16 * nc

    def order(to_heads):
        a = iota((n16, n16), 0)
        b = iota((n16, n16), 1)
        if not to_heads:
            a, b = b, a
        head, rest = a // prow, lax.rem(a, prow)
        return jnp.where(rest * KVH + head == b, 1.0, 0.0).astype(BF)

    to_heads = order(True)
    others(nc, c, lambda p: copy_a(p, p).wait_recv())
    my_rows = pl.ds(pl.multiple_of(r * prow, prow), prow)
    for w in range(2):
        got = jnp.concatenate([pown[j, w] for j in range(nc)], 0)
        mine = dot(to_heads, got).astype(BF)
        for g in range(KVH):
            kv[g, w, my_rows, :] = mine[g * prow:(g + 1) * prow]

    pieces = ((0, 1), (1, 2), (3, 5))

    def copy_b(n, slot, peer):
        g0, count = pieces[n]
        rows = pl.ds(pl.multiple_of(slot * prow, prow), prow)
        part = kv.at[pl.ds(g0, count), :, rows, :]
        return pltpu.make_async_remote_copy(
            src_ref=part, dst_ref=part,
            send_sem=b_send.at[n, peer], recv_sem=b_recv.at[n, slot],
            device_id={"resp": peer}, device_id_type=MESH)

    for n in range(len(pieces)):
        others(nr, r, lambda p: copy_b(n, r, p).start())

    load_q.wait()
    load_d.wait()

    def copy_t(g, block, src):
        return pltpu.make_async_remote_copy(
            src_ref=term.at[g, :, block_rows(block), :], dst_ref=rterm.at[src, g],
            send_sem=t_send.at[g, block], recv_sem=t_recv.at[g, src],
            device_id={"ctx": block}, device_id_type=MESH)

    def copy_p(n, owner, src):
        rows = pl.ds(pl.multiple_of(owner * prow, prow), prow)
        return pltpu.make_async_remote_copy(
            src_ref=term.at[pl.ds(2 * n, 2), :, rows, :], dst_ref=pterm.at[src, pl.ds(2 * n, 2)],
            send_sem=p_send.at[n, owner], recv_sem=p_recv.at[n, src],
            device_id={"resp": owner}, device_id_type=MESH)

    def store_out(g, which):
        cols = pl.ds(pl.multiple_of(g * ROWS, ROWS), ROWS)
        src, dst = ((ov, out_hbm), (dqv, dq_hbm))[which]
        return pltpu.make_async_copy(src.at[:, cols], dst.at[:, cols], out_sem.at[which, g])

    def head(g):
        for n, (g0, _) in enumerate(pieces):
            @pl.when(g == g0)
            def _():
                others(nr, r, lambda p: copy_b(n, p, p).wait_recv())
        loop(0, c, lambda j: copy_g(g, j, j).wait_recv())

        cols = [pl.ds(pl.multiple_of(g * ROWS + a * HD, HD), HD) for a in range(G)]
        k = kv[g, 0]
        v = kv[g, 1]
        q = jnp.concatenate([qv[:, x] for x in cols], 0)
        d = jnp.concatenate([jnp.where(live, dv[:, x], jnp.zeros((), BF)) for x in cols], 0)
        limit = jnp.concatenate([causal_cols[...]] * G, 0)
        s = dot_nt(jnp.concatenate([k, hidden_cols[...]], 1), jnp.concatenate([q, limit], 1))
        top = jnp.max(s, 0, keepdims=True)
        p = jnp.exp2((s - top) * (SCALE * LOG2E))
        inv = 1.0 / jnp.sum(p, 0, keepdims=True)
        p = p.astype(BF)
        out = dot(v.T, p) * (inv * jnp.concatenate([live_lane] * G, 1))
        out = out.T.astype(BF)
        for a in range(G):
            ov[:, cols[a]] = out[a * TOK:(a + 1) * TOK]
        store_out(g, 0).start()
        corr = -jnp.sum(d.astype(F32) * out.astype(F32), 1, keepdims=True)
        high = corr.astype(BF).astype(F32)
        lane = iota((ROWS, HD), 1)
        corr_cols = jnp.where(lane == 0, high, jnp.where(lane == 1, corr - high, 0.0)).astype(BF)
        dp = dot_nt(jnp.concatenate([v, ones_cols[...]], 1), jnp.concatenate([d, corr_cols], 1))
        ds = (p.astype(F32) * dp).astype(BF)
        dq = (dot(k.T, ds) * (inv * SCALE)).T.astype(BF)
        for a in range(G):
            dqv[:, cols[a]] = dq[a * TOK:(a + 1) * TOK]
        store_out(g, 1).start()
        inv_col = jnp.broadcast_to(inv, (HD, ROWS)).T
        term[g, 1] = dot(p, (d.astype(F32) * inv_col).astype(BF)).astype(BF)
        term[g, 0] = dot(ds, (q.astype(F32) * (inv_col * SCALE)).astype(BF)).astype(BF)
        loop(0, c, lambda j: copy_t(g, j, c).start())
        for n in range(KVH // 2):
            @pl.when(g == 2 * n + 1)
            def _():
                others(nr, r, lambda p: copy_p(n, p, r).start())

    loop(0, KVH, head)

    for n in range(KVH // 2):
        others(nr, r, lambda p: copy_p(n, r, p).wait_recv())
    psum[...] = term[:, :, my_rows, :].astype(F32)

    def add_p(p):
        psum[...] += pterm[p].astype(F32)

    others(nr, r, add_p)
    from_heads = order(False)
    for w in range(2):
        part = jnp.concatenate([psum[g, w] for g in range(KVH)], 0).astype(BF)
        part = dot(from_heads, part).astype(BF)
        for j in range(nc):
            prep[j, w] = part[16 * j:16 * (j + 1)]

    def copy_z(owner, src):
        return pltpu.make_async_remote_copy(
            src_ref=prep.at[owner], dst_ref=pback.at[src],
            send_sem=z_send.at[owner], recv_sem=z_recv.at[src],
            device_id={"ctx": owner}, device_id_type=MESH)

    others(nc, c, lambda p: copy_z(p, c).start())

    def sum_head(g):
        gcol = pl.ds(pl.multiple_of(g * HD, HD), HD)
        kg_ref[:, gcol] = term[g, 0, block_rows(c), :].astype(F32)
        vg_ref[:, gcol] = term[g, 1, block_rows(c), :].astype(F32)

        def add(src):
            copy_t(g, c, src).wait_recv()
            kg_ref[:, gcol] += rterm[src, g, 0].astype(F32)
            vg_ref[:, gcol] += rterm[src, g, 1].astype(F32)

        loop(c + 1, nc, add)

    loop(0, KVH, sum_head)

    others(nc, c, lambda p: copy_z(c, p).wait_recv())
    pkg_ref[...] = prep[c, 0].astype(F32)
    pvg_ref[...] = prep[c, 1].astype(F32)

    def add_z(p):
        pkg_ref[...] += pback[p, 0].astype(F32)
        pvg_ref[...] += pback[p, 1].astype(F32)

    others(nc, c, add_z)

    others(nc, c, lambda p: copy_a(c, p).wait_send())
    for n in range(len(pieces)):
        others(nr, r, lambda p: copy_b(n, r, p).wait_send())
    for n in range(KVH // 2):
        others(nr, r, lambda p: copy_p(n, p, r).wait_send())
    others(nc, c, lambda p: copy_z(p, c).wait_send())

    def finish(g):
        loop(c + 1, nc, lambda p: copy_g(g, c, p).wait_send())
        loop(0, c, lambda j: copy_t(g, j, c).wait_send())
        store_out(g, 0).wait()
        store_out(g, 1).wait()

    loop(0, KVH, finish)


def per_device(
    nr, nc, queries, resp_keys, resp_values, prompt_keys, prompt_values, upstream, lengths, prompt_length
):
    prow = 2 * nc
    key_rows = nr * prow + nc * TOK
    width = KVH * HD
    vmem = pl.BlockSpec(memory_space=pltpu.VMEM)
    smem = pl.BlockSpec(memory_space=pltpu.SMEM)
    hbm = pl.BlockSpec(memory_space=pl.ANY)
    dma = pltpu.SemaphoreType.DMA
    big = jax.ShapeDtypeStruct((TOK, KVH * ROWS), BF)
    grad = jax.ShapeDtypeStruct((TOK, width), F32)
    small = jax.ShapeDtypeStruct((16, HD), F32)
    outs = pl.pallas_call(
        functools.partial(kernel, nr, nc),
        out_shape=(big, big, grad, grad, small, small),
        in_specs=[hbm, hbm, vmem, vmem, vmem, vmem, smem, smem],
        out_specs=[hbm, hbm, vmem, vmem, vmem, vmem],
        scratch_shapes=[
            pltpu.VMEM((TOK, KVH * ROWS), BF),
            pltpu.VMEM((TOK, KVH * ROWS), BF),
            pltpu.VMEM((TOK, KVH * ROWS), BF),
            pltpu.VMEM((TOK, KVH * ROWS), BF),
            pltpu.VMEM((KVH, 2, key_rows, HD), BF),
            pltpu.VMEM((KVH, 2, key_rows, HD), BF),
            pltpu.VMEM((nc, KVH, 2, TOK, HD), BF),
            pltpu.VMEM((key_rows, HD), BF),
            pltpu.VMEM((key_rows, HD), BF),
            pltpu.VMEM((TOK, HD), BF),
            pltpu.VMEM((nc, 2, 16, HD), BF),
            pltpu.VMEM((nc, 2, 16, HD), BF),
            pltpu.VMEM((nr, KVH, 2, prow, HD), BF),
            pltpu.VMEM((KVH, 2, prow, HD), F32),
            pltpu.VMEM((nc, 2, 16, HD), BF),
            dma((2,)), dma((2, KVH)),
            dma((nc,)), dma((nc,)), dma((3, nr)), dma((3, nr)),
            dma((KVH, nc)), dma((KVH, nc)),
            dma((KVH, nc)), dma((KVH, nc)),
            dma((KVH // 2, nr)), dma((KVH // 2, nr)),
            dma((nc,)), dma((nc,)),
        ],
        compiler_params=pltpu.CompilerParams(
            collective_id=0, has_side_effects=True, vmem_limit_bytes=60 * 2**20),
        cost_estimate=pl.CostEstimate(
            flops=12 * KVH * ROWS * key_rows * HD, bytes_accessed=10 * 2**20,
            transcendentals=KVH * ROWS * key_rows),
    )(
        queries[0], upstream[0], resp_keys[0], resp_values[0],
        prompt_keys.reshape(16, HD), prompt_values.reshape(16, HD), lengths, prompt_length,
    )
    attended, query_grads, key_grads, value_grads, pkg, pvg = outs
    return (
        attended[None], query_grads[None], key_grads[None], value_grads[None],
        pkg.reshape(2, width), pvg.reshape(2, width),
    )


def solution(mesh):
    tokens = P("resp", "ctx", None)
    rows = P(("resp", "ctx"), None)
    return jax.shard_map(
        functools.partial(per_device, mesh.shape["resp"], mesh.shape["ctx"]),
        mesh=mesh,
        in_specs=(tokens, tokens, tokens, rows, rows, tokens, P("resp"), P()),
        out_specs=(tokens, tokens, tokens, tokens, rows, rows),
        check_vma=False,
    )
```

time: 1130 us -> 130 us (0.12)
  blocking collectives: 654 us -> 0 us
  waiting for transfers between devices: 242 us -> 0 us
  Pallas kernels: 0 us -> 115 us
  matrix products: 109 us -> 0 us
  other arithmetic: 56.1 us -> 0 us
  local copies, waits for them, and re-layouts: 51.6 us -> 11.4 us
  between operations: 15.2 us -> 1.94 us
    all_gather x2 -> x0, blocking collectives: 654 us -> none  [the longest x1 333 us: per_device(): lax.all_gather(prompt_keys, ('resp', 'ctx'), axis=0, tiled=True)]
    unnamed x6 -> x0, waiting for transfers between devices: 139 us -> none
    pallas_call x0 -> x1, Pallas kernels: none -> 115 us  [per_device(): pl.pallas_call(functools.partial(kernel, nr, nc), out_shape=(big, big, gr...]
    reduce_scatter x2 -> x0, waiting for transfers between devices: 102 us -> none  [the longest x1 52.2 us: per_device(): lax.psum_scatter(key_terms[prompt_rows:].astype(jnp.bfloat16), 'ctx', sca...]
    dot_general x40 -> x0, matrix products: 74.5 us -> none  [the longest x8 21.5 us: one_group(): jnp.einsum('tjd,kd->tjk', ggroup, vgroup, preferred_element_type=jnp.floa...]
    sub x8 -> x0, matrix products: 34.3 us -> none  [one_group(): expo = jnp.exp(scores - top)]
    convert_element_type x8 -> x0, other arithmetic: 30.8 us -> none  [one_group(): weights_low = weights.astype(jnp.bfloat16)]
    slice x4 -> x0, local copies, waits for them, and re-layouts: 12.4 us -> none  [the longest x1 3.88 us: per_device(): key_terms[prompt_rows:].astype(jnp.bfloat16)]
  transfers between devices with their start and end apart: 5 -> 0, of which waited for: 3 -> 0; matrix products, arithmetic and copies ran while one was open for 2% -> 0% of each run, Pallas kernels for 0% -> 0%
where the time goes in v1:
time: 130 us; the launch traced here: 129 us
  Pallas kernels  115 us (88%)
  local copies, waits for them, and re-layouts  11.4 us (9%)
  between operations  1.94 us (1%)
    pallas_call x1, Pallas kernels, per_device(): pl.pallas_call(functools.partial(kernel, nr, nc), out_shape=(big, big, gr...  115 us
    unnamed x10, local copies, waits for them, and re-layouts  6.21 us

profile of v1, /device:TPU:0, one launch (start us, length us, event | category | flops | bytes accessed | tf_op | source)
XLA Modules:
  0.0 128.8 jit_solution(4300130488129948020)
XLA Ops:
  1.9 1.3 %reshape.24.pk_ref = bf16[16,128]{1,0:T(8,128)(2,1)} reshape(bf16[2,1024]{1,0:T(2,128)(2,1)} %param.11) | data formatting | bytes 8192 | tf_op jit(solution)/shard_map/reshape | solution.py:332
  3.2 1.3 %reshape.25.pv_ref = bf16[16,128]{1,0:T(8,128)(2,1)} reshape(bf16[2,1024]{1,0:T(2,128)(2,1)} %param.12) | data formatting | bytes 8192 | tf_op jit(solution)/shard_map/reshape | solution.py:332
  4.5 115.5 %shard_map.127 = (bf16[128,8192]{1,0:T(8,128)(2,1)}, bf16[128,8192]{1,0:T(8,128)(2,1)}, f32[128,1024]{1,0:T(8,128)}, f32[128,1024]{1,0:T(8,128)}, f32[16,128]{1,0:T(8,128)}, /*index=5*/f32[16,128]{1,0:T(8,128)}) custom-call(bf16[128,8192]{1,0:T(8,128)(2,1)} %bitcast.12, bf16[128,8192]{1,0:T(8,128)(2,1)} %bitcast.13, bf16[128,1024]{1,0:T(8,128)(2,1)} %bitcast.14, ...), custom_call_target="tpu_custom_call" | custom-call | flops 16106127360 | bytes 10485760 | tf_op jit(solution)/shard_map/pallas_call | solution.py:297
  120.0 1.3 %reshape.26 = f32[2,1024]{1,0:T(2,128)} reshape(f32[16,128]{1,0:T(8,128)} %get-tuple-element.16) | data formatting | bytes 16384 | tf_op jit(solution)/shard_map/reshape | solution.py:337
  121.3 1.3 %reshape.27 = f32[2,1024]{1,0:T(2,128)} reshape(f32[16,128]{1,0:T(8,128)} %get-tuple-element.17) | data formatting | bytes 16384 | tf_op jit(solution)/shard_map/reshape | solution.py:337
  122.6 0.0 copy-start
  122.6 3.2 %copy.20 = bf16[1,128,8192]{2,1,0:T(8,128)(2,1)} copy(bf16[1,128,8192]{2,1,0:T(8,128)(2,1)} %bitcast.9) | data formatting | bytes 4194304
  125.8 0.0 copy-done
  125.8 0.0 copy-start.2
  125.8 0.0 copy-start.1
  125.9 1.3 %copy.21 = bf16[1,128,8192]{2,1,0:T(8,128)(2,1)} copy(bf16[1,128,8192]{2,1,0:T(8,128)(2,1)S(1)} %bitcast.8) | data formatting | bytes 4194304
  127.2 0.1 copy-done.2
  127.2 0.8 copy.22
  128.0 0.0 copy-done.1
  128.0 0.8 copy.23
Async XLA Ops:
  122.6 3.2 %copy-start = (bf16[128,8192]{1,0:T(8,128)(2,1)S(1)}, bf16[128,8192]{1,0:T(8,128)(2,1)}, u32[]{:S(2)}) copy-start(bf16[128,8192]{1,0:T(8,128)(2,1)} %get-tuple-element.13) | copy-start | bytes 6291460
  125.8 1.4 %copy-start.2 = (f32[128,1024]{1,0:T(8,128)S(1)}, f32[128,1024]{1,0:T(8,128)}, u32[]{:S(2)}) copy-start(f32[128,1024]{1,0:T(8,128)} %get-tuple-element.14) | copy-start | bytes 1572868
  125.8 2.2 %copy-start.1 = (f32[128,1024]{1,0:T(8,128)S(1)}, f32[128,1024]{1,0:T(8,128)}, u32[]{:S(2)}) copy-start(f32[128,1024]{1,0:T(8,128)} %get-tuple-element.15) | copy-start | bytes 1572868

commit v2 on v1

v2 whole, which is shorter than its diff:
```python
import functools

import jax
import jax.numpy as jnp
from jax import lax
from jax.experimental import pallas as pl
from jax.experimental.pallas import tpu as pltpu
from jax.sharding import PartitionSpec as P

HD = 128
KVH = 8
G = 8
ROWS = G * HD
TOK = 128
SCALE = HD**-0.5
LOG2E = 1.4426950408889634
HIDE = -1e30
NT = (((1,), (1,)), ((), ()))
F32 = jnp.float32
BF = jnp.bfloat16
MESH = pl.DeviceIdType.MESH

PROMPT_IN = ((0, 1), (1, 2), (3, 5))
PROMPT_OUT = ((0, 4), (4, 3), (7, 1))
GATHER = ((0, 1), (1, 1), (2, 2), (4, 2), (6, 2))
TERMS = tuple((g, 1) for g in range(8))


def iota(shape, axis):
    return lax.broadcasted_iota(jnp.int32, shape, axis)


def dot(a, b):
    return jnp.dot(a, b, preferred_element_type=F32)


def dot_nt(a, b):
    return lax.dot_general(a, b, NT, preferred_element_type=F32)


def kernel(
    nr, nc,
    q_hbm, d_hbm, k_ref, v_ref, pk_ref, pv_ref, len_ref, plen_ref,
    out_hbm, dq_hbm, kg_ref, vg_ref, pkg_ref, pvg_ref,
    qv, dv, ov, dqv, kv, term, rterm, hidden_cols, ones_cols, causal_cols,
    pown, prep, pterm, psum, xsend, xrecv, pback,
    in_sem, out_sem, x_sem,
    a_send, a_recv, b_send, b_recv, g_send, g_recv,
    t_send, t_recv, p_send, p_recv, z_send, z_recv,
):
    prow = 2 * nc
    prompt = nr * prow
    key_rows = prompt + nc * TOK
    r = lax.axis_index("resp")
    c = lax.axis_index("ctx")
    nm = nr // 2
    half = lax.rem(r // 2, 2)
    m = (r // 4) * 2 + lax.rem(r, 2)
    partner = r + 2 - 4 * half

    def resp_of(pair):
        return (pair // 2) * 4 + 2 * half + lax.rem(pair, 2)

    load_q = pltpu.make_async_copy(q_hbm, qv, in_sem.at[0])
    load_d = pltpu.make_async_copy(d_hbm, dv, in_sem.at[1])
    load_q.start()
    load_d.start()

    barrier = pltpu.get_barrier_semaphore()

    def others(n, me, body):
        def step(i, carry):
            body(lax.rem(me + i, n))
            return carry

        lax.fori_loop(1, n, step, 0)

    others(nc, c, lambda p: pl.semaphore_signal(barrier, inc=1, device_id={"ctx": p}, device_id_type=MESH))
    others(nm, m, lambda p: pl.semaphore_signal(
        barrier, inc=1, device_id={"resp": resp_of(p)}, device_id_type=MESH))
    pl.semaphore_signal(barrier, inc=1, device_id={"resp": partner}, device_id_type=MESH)

    def block_rows(j):
        return pl.ds(pl.multiple_of(prompt + j * TOK, TOK), TOK)

    for w, ref in enumerate((pk_ref, pv_ref)):
        wide = ref[...].astype(F32)
        rows = [wide[:, g * HD:(g + 1) * HD] for g in range(KVH)]
        pown[half, c, w] = jnp.concatenate(rows, 0).astype(BF)
    for g in range(KVH):
        kv[g, 0, block_rows(c), :] = k_ref[:, g * HD:(g + 1) * HD]
        kv[g, 1, block_rows(c), :] = v_ref[:, g * HD:(g + 1) * HD]

    pl.semaphore_wait(barrier, nc - 1 + nm)

    def copy_a(slot, peer):
        return pltpu.make_async_remote_copy(
            src_ref=pown.at[half, slot], dst_ref=pown.at[half, slot],
            send_sem=a_send.at[peer], recv_sem=a_recv.at[slot],
            device_id={"ctx": peer}, device_id_type=MESH)

    others(nc, c, lambda p: copy_a(c, p).start())

    def copy_g(n, slot, peer):
        g0, count = GATHER[n]
        part = kv.at[pl.ds(g0, count), :, block_rows(slot), :]
        return pltpu.make_async_remote_copy(
            src_ref=part, dst_ref=part,
            send_sem=g_send.at[n, peer], recv_sem=g_recv.at[n, slot],
            device_id={"ctx": peer}, device_id_type=MESH)

    def loop(lo, hi, body):
        def step(i, carry):
            body(i)
            return carry

        lax.fori_loop(lo, hi, step, 0)

    def gather(n):
        loop(c + 1, nc, lambda p: copy_g(n, c, p).start())

    gather(0)
    gather(1)
    gather(2)

    def clear(j):
        def one(g):
            kv[g, 0, block_rows(j), :] = jnp.zeros((TOK, HD), BF)
            kv[g, 1, block_rows(j), :] = jnp.zeros((TOK, HD), BF)
        loop(0, KVH, one)

    loop(c + 1, nc, clear)

    row = iota((key_rows, HD), 0)
    col = iota((key_rows, HD), 1)
    slot, within = row // prow, lax.rem(row, prow)
    place = ((slot // 4) * 4 + lax.rem(slot, 2) * 2 + lax.rem(slot // 2, 2)) * prow + within
    gone = ((row < prompt) & (place >= plen_ref[0])) | (row >= prompt + (c + 1) * TOK)
    diagonal = (row - (prompt + c * TOK) == col) & (col > 0)
    hidden_cols[...] = jnp.where(diagonal, 1.0, jnp.where(gone & (col == 0), HIDE, 0.0)).astype(BF)
    ones_cols[...] = jnp.where(col < 2, 1.0, 0.0).astype(BF)
    tok = iota((TOK, HD), 0)
    key = iota((TOK, HD), 1)
    causal_cols[...] = jnp.where(key == 0, 1.0, jnp.where(key > tok, HIDE, 0.0)).astype(BF)
    live = c * TOK + tok < len_ref[0]
    live_lane = jnp.where(c * TOK + iota((1, TOK), 1) < len_ref[0], 1.0, 0.0)

    n16 = 16 * nc

    def order(to_heads):
        a = iota((n16, n16), 0)
        b = iota((n16, n16), 1)
        if not to_heads:
            a, b = b, a
        head, rest = a // prow, lax.rem(a, prow)
        return jnp.where((rest // 2) * 16 + head * 2 + lax.rem(rest, 2) == b, 1.0, 0.0).astype(BF)

    def copy_x(which, src, dst):
        return pltpu.make_async_remote_copy(
            src_ref=src, dst_ref=dst, send_sem=x_sem.at[which, 0], recv_sem=x_sem.at[which, 1],
            device_id={"resp": partner}, device_id_type=MESH)

    to_heads = order(True)
    others(nc, c, lambda p: copy_a(p, p).wait_recv())
    swap = copy_x(0, pown.at[half], pown.at[half])
    swap.start()
    swap.wait_recv()

    def pair_rows(pair, h=0, count=2):
        return pl.ds(pl.multiple_of((2 * pair + h) * prow, prow), count * prow)

    for h in range(2):
        for w in range(2):
            got = jnp.concatenate([pown[h, j, w] for j in range(nc)], 0)
            mine = dot(to_heads, got).astype(BF)
            for g in range(KVH):
                kv[g, w, pair_rows(m, h, 1), :] = mine[g * prow:(g + 1) * prow]

    def copy_b(n, slot, peer):
        g0, count = PROMPT_IN[n]
        part = kv.at[pl.ds(g0, count), :, pair_rows(slot), :]
        return pltpu.make_async_remote_copy(
            src_ref=part, dst_ref=part,
            send_sem=b_send.at[n, peer], recv_sem=b_recv.at[n, slot],
            device_id={"resp": resp_of(peer)}, device_id_type=MESH)

    for n in range(len(PROMPT_IN)):
        others(nm, m, lambda p: copy_b(n, m, p).start())

    load_q.wait()
    load_d.wait()

    def copy_t(n, block, src):
        g0, count = TERMS[n]
        return pltpu.make_async_remote_copy(
            src_ref=term.at[pl.ds(g0, count), :, block_rows(block), :],
            dst_ref=rterm.at[src, pl.ds(g0, count)],
            send_sem=t_send.at[n, block], recv_sem=t_recv.at[n, src],
            device_id={"ctx": block}, device_id_type=MESH)

    def copy_p(n, owner, src):
        g0, count = PROMPT_OUT[n]
        return pltpu.make_async_remote_copy(
            src_ref=term.at[pl.ds(g0, count), :, pair_rows(owner), :],
            dst_ref=pterm.at[src, pl.ds(g0, count)],
            send_sem=p_send.at[n, owner], recv_sem=p_recv.at[n, src],
            device_id={"resp": resp_of(owner)}, device_id_type=MESH)

    def store_out(g, which):
        cols = pl.ds(pl.multiple_of(g * ROWS, ROWS), ROWS)
        src, dst = ((ov, out_hbm), (dqv, dq_hbm))[which]
        return pltpu.make_async_copy(src.at[:, cols], dst.at[:, cols], out_sem.at[which, g])

    def head(g):
        for n, (g0, _) in enumerate(PROMPT_IN):
            @pl.when(g == g0)
            def _():
                others(nm, m, lambda p: copy_b(n, p, p).wait_recv())
        for n, (g0, _) in enumerate(GATHER):
            @pl.when(g == g0)
            def _():
                loop(0, c, lambda j: copy_g(n, j, j).wait_recv())
            if n >= 3:
                @pl.when(g == g0 - 4)
                def _():
                    gather(n)

        cols = [pl.ds(pl.multiple_of(g * ROWS + a * HD, HD), HD) for a in range(G)]
        k = kv[g, 0]
        v = kv[g, 1]
        q = jnp.concatenate([qv[:, x] for x in cols], 0)
        d = jnp.concatenate([jnp.where(live, dv[:, x], jnp.zeros((), BF)) for x in cols], 0)
        limit = jnp.concatenate([causal_cols[...]] * G, 0)
        s = dot_nt(jnp.concatenate([k, hidden_cols[...]], 1), jnp.concatenate([q, limit], 1))
        top = jnp.max(s, 0, keepdims=True)
        p = jnp.exp2((s - top) * (SCALE * LOG2E))
        inv = 1.0 / jnp.sum(p, 0, keepdims=True)
        p = p.astype(BF)
        out = dot(v.T, p) * (inv * jnp.concatenate([live_lane] * G, 1))
        out = out.T.astype(BF)
        for a in range(G):
            ov[:, cols[a]] = out[a * TOK:(a + 1) * TOK]
        store_out(g, 0).start()
        corr = -jnp.sum(d.astype(F32) * out.astype(F32), 1, keepdims=True)
        high = corr.astype(BF).astype(F32)
        lane = iota((ROWS, HD), 1)
        corr_cols = jnp.where(lane == 0, high, jnp.where(lane == 1, corr - high, 0.0)).astype(BF)
        dp = dot_nt(jnp.concatenate([v, ones_cols[...]], 1), jnp.concatenate([d, corr_cols], 1))
        ds = (p.astype(F32) * dp).astype(BF)
        dq = (dot(k.T, ds) * (inv * SCALE)).T.astype(BF)
        for a in range(G):
            dqv[:, cols[a]] = dq[a * TOK:(a + 1) * TOK]
        store_out(g, 1).start()
        inv_col = jnp.broadcast_to(inv, (HD, ROWS)).T
        term[g, 1] = dot(p, (d.astype(F32) * inv_col).astype(BF)).astype(BF)
        term[g, 0] = dot(ds, (q.astype(F32) * (inv_col * SCALE)).astype(BF)).astype(BF)
        for n, (g0, count) in enumerate(TERMS):
            @pl.when(g == g0 + count - 1)
            def _():
                loop(0, c, lambda j: copy_t(n, j, c).start())
        for n, (g0, count) in enumerate(PROMPT_OUT):
            @pl.when(g == g0 + count - 1)
            def _():
                others(nm, m, lambda p: copy_p(n, p, m).start())

    loop(0, KVH, head)

    for n in range(len(PROMPT_OUT)):
        others(nm, m, lambda p: copy_p(n, m, p).wait_recv())
    for h in range(2):
        psum[h] = term[:, :, pair_rows(m, h, 1), :].astype(F32)

    def add_p(p):
        for h in range(2):
            psum[h] += pterm[p, :, :, h * prow:(h + 1) * prow, :].astype(F32)

    others(nm, m, add_p)
    xsend[...] = psum[1 - half].astype(BF)
    swap_back = copy_x(1, xsend, xrecv)
    swap_back.start()
    swap_back.wait_recv()
    psum[half] += xrecv[...].astype(F32)
    from_heads = order(False)
    for w in range(2):
        part = jnp.concatenate([psum[half, g, w] for g in range(KVH)], 0).astype(BF)
        part = dot(from_heads, part).astype(BF)
        for j in range(nc):
            prep[j, w] = part[16 * j:16 * (j + 1)]

    def copy_z(owner, src):
        return pltpu.make_async_remote_copy(
            src_ref=prep.at[owner], dst_ref=pback.at[src],
            send_sem=z_send.at[owner], recv_sem=z_recv.at[src],
            device_id={"ctx": owner}, device_id_type=MESH)

    others(nc, c, lambda p: copy_z(p, c).start())

    for n, (g0, count) in enumerate(TERMS):
        loop(c + 1, nc, lambda src: copy_t(n, c, src).wait_recv())
        for g in range(g0, g0 + count):
            for w, ref in enumerate((kg_ref, vg_ref)):
                ref[:, g * HD:(g + 1) * HD] = lax.fori_loop(
                    c + 1, nc, lambda src, total: total + rterm[src, g, w].astype(F32),
                    term[g, w, block_rows(c), :].astype(F32))

    others(nc, c, lambda p: copy_z(c, p).wait_recv())
    for w, ref in enumerate((pkg_ref, pvg_ref)):
        total = prep[c, w].astype(F32)
        for i in range(1, nc):
            total += pback[lax.rem(c + i, nc), w].astype(F32)
        for g in range(KVH):
            ref[:, g * HD:(g + 1) * HD] = total[2 * g:2 * g + 2]

    others(nc, c, lambda p: copy_a(c, p).wait_send())
    swap.wait_send()
    swap_back.wait_send()
    for n in range(len(PROMPT_IN)):
        others(nm, m, lambda p: copy_b(n, m, p).wait_send())
    for n in range(len(PROMPT_OUT)):
        others(nm, m, lambda p: copy_p(n, p, m).wait_send())
    others(nc, c, lambda p: copy_z(p, c).wait_send())
    for n in range(len(GATHER)):
        loop(c + 1, nc, lambda p: copy_g(n, c, p).wait_send())
    for n in range(len(TERMS)):
        loop(0, c, lambda j: copy_t(n, j, c).wait_send())

    def finish(g):
        store_out(g, 0).wait()
        store_out(g, 1).wait()

    loop(0, KVH, finish)


def per_device(
    nr, nc, queries, resp_keys, resp_values, prompt_keys, prompt_values, upstream, lengths, prompt_length
):
    prow = 2 * nc
    key_rows = nr * prow + nc * TOK
    width = KVH * HD
    vmem = pl.BlockSpec(memory_space=pltpu.VMEM)
    smem = pl.BlockSpec(memory_space=pltpu.SMEM)
    hbm = pl.BlockSpec(memory_space=pl.ANY)
    dma = pltpu.SemaphoreType.DMA
    big = jax.ShapeDtypeStruct((TOK, KVH * ROWS), BF)
    grad = jax.ShapeDtypeStruct((TOK, width), F32)
    small = jax.ShapeDtypeStruct((2, width), F32)
    outs = pl.pallas_call(
        functools.partial(kernel, nr, nc),
        out_shape=(big, big, grad, grad, small, small),
        in_specs=[hbm, hbm, vmem, vmem, vmem, vmem, smem, smem],
        out_specs=[hbm, hbm, vmem, vmem, vmem, vmem],
        scratch_shapes=[
            pltpu.VMEM((TOK, KVH * ROWS), BF),
            pltpu.VMEM((TOK, KVH * ROWS), BF),
            pltpu.VMEM((TOK, KVH * ROWS), BF),
            pltpu.VMEM((TOK, KVH * ROWS), BF),
            pltpu.VMEM((KVH, 2, key_rows, HD), BF),
            pltpu.VMEM((KVH, 2, key_rows, HD), BF),
            pltpu.VMEM((nc, KVH, 2, TOK, HD), BF),
            pltpu.VMEM((key_rows, HD), BF),
            pltpu.VMEM((key_rows, HD), BF),
            pltpu.VMEM((TOK, HD), BF),
            pltpu.VMEM((2, nc, 2, 16, HD), BF),
            pltpu.VMEM((nc, 2, 16, HD), BF),
            pltpu.VMEM((nr // 2, KVH, 2, 2 * prow, HD), BF),
            pltpu.VMEM((2, KVH, 2, prow, HD), F32),
            pltpu.VMEM((KVH, 2, prow, HD), BF),
            pltpu.VMEM((KVH, 2, prow, HD), BF),
            pltpu.VMEM((nc, 2, 16, HD), BF),
            dma((2,)), dma((2, KVH)), dma((2, 2)),
            dma((nc,)), dma((nc,)),
            dma((len(PROMPT_IN), nr // 2)), dma((len(PROMPT_IN), nr // 2)),
            dma((len(GATHER), nc)), dma((len(GATHER), nc)),
            dma((len(TERMS), nc)), dma((len(TERMS), nc)),
            dma((len(PROMPT_OUT), nr // 2)), dma((len(PROMPT_OUT), nr // 2)),
            dma((nc,)), dma((nc,)),
        ],
        compiler_params=pltpu.CompilerParams(
            collective_id=0, has_side_effects=True, vmem_limit_bytes=60 * 2**20),
        cost_estimate=pl.CostEstimate(
            flops=12 * KVH * ROWS * key_rows * HD, bytes_accessed=10 * 2**20,
            transcendentals=KVH * ROWS * key_rows),
    )(
        queries[0], upstream[0], resp_keys[0], resp_values[0],
        prompt_keys, prompt_values, lengths, prompt_length,
    )
    attended, query_grads, key_grads, value_grads, pkg, pvg = outs
    return (
        attended[None], query_grads[None], key_grads[None], value_grads[None],
        pkg, pvg,
    )


def solution(mesh):
    tokens = P("resp", "ctx", None)
    rows = P(("resp", "ctx"), None)
    return jax.shard_map(
        functools.partial(per_device, mesh.shape["resp"], mesh.shape["ctx"]),
        mesh=mesh,
        in_specs=(tokens, tokens, tokens, rows, rows, tokens, P("resp"), P()),
        out_specs=(tokens, tokens, tokens, tokens, rows, rows),
        check_vma=False,
    )
```

time: 130 us -> 105 us (0.81)
  Pallas kernels: 115 us -> 94.1 us
  local copies, waits for them, and re-layouts: 11.4 us -> 7.41 us
    pallas_call x1, Pallas kernels: 115 us -> 94.1 us  [per_device(): pl.pallas_call(functools.partial(kernel, nr, nc), out_shape=(big, big, gr...]
    reshape x4 -> x0, local copies, waits for them, and re-layouts: 5.19 us -> none  [the longest x1 1.3 us: per_device(): pkg.reshape(2, width)]
    unnamed x10 -> x16, local copies, waits for them, and re-layouts: 6.21 us -> 7.41 us
where the time goes in v2:
time: 105 us; the launch traced here: 103 us
  Pallas kernels  94.1 us (90%)
  local copies, waits for them, and re-layouts  7.41 us (7%)
  between operations  1.95 us (2%)
    pallas_call x1, Pallas kernels, per_device(): pl.pallas_call(functools.partial(kernel, nr, nc), out_shape=(big, big, gr...  94.1 us
    unnamed x16, local copies, waits for them, and re-layouts  7.41 us

profile of v2, /device:TPU:0, one launch (start us, length us, event | category | flops | bytes accessed | tf_op | source)
XLA Modules:
  0.0 103.5 jit_solution(10173379326008010279)
XLA Ops:
  1.9 94.1 %shard_map.127 = (bf16[128,8192]{1,0:T(8,128)(2,1)}, bf16[128,8192]{1,0:T(8,128)(2,1)}, f32[128,1024]{1,0:T(8,128)}, f32[128,1024]{1,0:T(8,128)}, f32[2,1024]{1,0:T(2,128)}, /*index=5*/f32[2,1024]{1,0:T(2,128)}) custom-call(bf16[128,8192]{1,0:T(8,128)(2,1)} %bitcast.12, bf16[128,8192]{1,0:T(8,128)(2,1)} %bitcast.13, bf16[128,1024]{1,0:T(8,128)(2,1)} %bitcast.14, ...), custom_call_target="tpu_custom_call" | custom-call | flops 16106127360 | bytes 10485760 | tf_op jit(solution)/shard_map/pallas_call | solution.py:347
  96.0 0.0 copy-start
  96.0 3.2 %copy.22 = bf16[1,128,8192]{2,1,0:T(8,128)(2,1)} copy(bf16[1,128,8192]{2,1,0:T(8,128)(2,1)} %bitcast.9) | data formatting | bytes 4194304
  99.3 0.0 copy-done
  99.3 0.0 copy-start.2
  99.3 0.0 copy-start.1
  99.3 1.3 %copy.23 = bf16[1,128,8192]{2,1,0:T(8,128)(2,1)} copy(bf16[1,128,8192]{2,1,0:T(8,128)(2,1)S(1)} %bitcast.8) | data formatting | bytes 4194304
  100.6 0.1 copy-done.2
  100.7 0.0 copy-start.4
  100.7 0.0 copy-start.3
  100.7 0.8 copy.24
  101.5 0.0 copy-done.1
  101.5 0.8 copy.25
  102.3 0.0 copy-done.4
  102.3 0.6 copy.26
  102.9 0.0 copy-done.3
  102.9 0.6 copy.27
Async XLA Ops:
  96.0 3.3 %copy-start = (bf16[128,8192]{1,0:T(8,128)(2,1)S(1)}, bf16[128,8192]{1,0:T(8,128)(2,1)}, u32[]{:S(2)}) copy-start(bf16[128,8192]{1,0:T(8,128)(2,1)} %get-tuple-element.13) | copy-start | bytes 6291460
  99.3 1.4 %copy-start.2 = (f32[128,1024]{1,0:T(8,128)S(1)}, f32[128,1024]{1,0:T(8,128)}, u32[]{:S(2)}) copy-start(f32[128,1024]{1,0:T(8,128)} %get-tuple-element.14) | copy-start | bytes 1572868
  99.3 2.2 %copy-start.1 = (f32[128,1024]{1,0:T(8,128)S(1)}, f32[128,1024]{1,0:T(8,128)}, u32[]{:S(2)}) copy-start(f32[128,1024]{1,0:T(8,128)} %get-tuple-element.15) | copy-start | bytes 1572868
  100.7 1.6 %copy-start.4 = (f32[2,1024]{1,0:T(2,128)S(1)}, f32[2,1024]{1,0:T(2,128)}, u32[]{:S(2)}) copy-start(f32[2,1024]{1,0:T(2,128)} %get-tuple-element.28) | copy-start | bytes 24580
  100.7 2.2 %copy-start.3 = (f32[2,1024]{1,0:T(2,128)S(1)}, f32[2,1024]{1,0:T(2,128)}, u32[]{:S(2)}) copy-start(f32[2,1024]{1,0:T(2,128)} %get-tuple-element.29) | copy-start | bytes 24580

commit v3 on v2

--- a/solution.py
+++ b/solution.py
@@ -22,7 +22,7 @@
 
 PROMPT_IN = ((0, 1), (1, 2), (3, 5))
 PROMPT_OUT = ((0, 4), (4, 3), (7, 1))
-GATHER = ((0, 1), (1, 1), (2, 2), (4, 2), (6, 2))
+GATHER = tuple((g, 1) for g in range(8))
 TERMS = tuple((g, 1) for g in range(8))
 
 
@@ -40,11 +40,11 @@
 
 def kernel(
     nr, nc,
-    q_hbm, d_hbm, k_ref, v_ref, pk_ref, pv_ref, len_ref, plen_ref,
-    out_hbm, dq_hbm, kg_ref, vg_ref, pkg_ref, pvg_ref,
-    qv, dv, ov, dqv, kv, term, rterm, hidden_cols, ones_cols, causal_cols,
+    q_hbm, d_hbm, k_hbm, v_hbm, pk_hbm, pv_hbm, len_ref, plen_ref,
+    ov, dqv, kg_ref, vg_ref, pkg_ref, pvg_ref,
+    qv, dv, k_ref, v_ref, pk_ref, pv_ref, kv, term, rterm, hidden_cols, causal_cols,
     pown, prep, pterm, psum, xsend, xrecv, pback,
-    in_sem, out_sem, x_sem,
+    in_sem, x_sem,
     a_send, a_recv, b_send, b_recv, g_send, g_recv,
     t_send, t_recv, p_send, p_recv, z_send, z_recv,
 ):
@@ -63,6 +63,12 @@
 
     load_q = pltpu.make_async_copy(q_hbm, qv, in_sem.at[0])
     load_d = pltpu.make_async_copy(d_hbm, dv, in_sem.at[1])
+    loads = [
+        pltpu.make_async_copy(src, dst, in_sem.at[2 + n])
+        for n, (src, dst) in enumerate(((pk_hbm, pk_ref), (pv_hbm, pv_ref), (k_hbm, k_ref), (v_hbm, v_ref)))
+    ]
+    for load in loads:
+        load.start()
     load_q.start()
     load_d.start()
 
@@ -83,6 +89,8 @@
     def block_rows(j):
         return pl.ds(pl.multiple_of(prompt + j * TOK, TOK), TOK)
 
+    for load in loads:
+        load.wait()
     for w, ref in enumerate((pk_ref, pv_ref)):
         wide = ref[...].astype(F32)
         rows = [wide[:, g * HD:(g + 1) * HD] for g in range(KVH)]
@@ -117,11 +125,8 @@
         lax.fori_loop(lo, hi, step, 0)
 
     def gather(n):
-        loop(c + 1, nc, lambda p: copy_g(n, c, p).start())
-
-    gather(0)
-    gather(1)
-    gather(2)
+        loop(0, nc - 1 - c, lambda i: copy_g(n, c, nc - 1 - i).start())
+
 
     def clear(j):
         def one(g):
@@ -138,7 +143,6 @@
     gone = ((row < prompt) & (place >= plen_ref[0])) | (row >= prompt + (c + 1) * TOK)
     diagonal = (row - (prompt + c * TOK) == col) & (col > 0)
     hidden_cols[...] = jnp.where(diagonal, 1.0, jnp.where(gone & (col == 0), HIDE, 0.0)).astype(BF)
-    ones_cols[...] = jnp.where(col < 2, 1.0, 0.0).astype(BF)
     tok = iota((TOK, HD), 0)
     key = iota((TOK, HD), 1)
     causal_cols[...] = jnp.where(key == 0, 1.0, jnp.where(key > tok, HIDE, 0.0)).astype(BF)
@@ -162,9 +166,11 @@
 
     to_heads = order(True)
     others(nc, c, lambda p: copy_a(p, p).wait_recv())
+    gather(0)
     swap = copy_x(0, pown.at[half], pown.at[half])
     swap.start()
     swap.wait_recv()
+    gather(1)
 
     def pair_rows(pair, h=0, count=2):
         return pl.ds(pl.multiple_of((2 * pair + h) * prow, prow), count * prow)
@@ -184,8 +190,10 @@
             send_sem=b_send.at[n, peer], recv_sem=b_recv.at[n, slot],
             device_id={"resp": resp_of(peer)}, device_id_type=MESH)
 
-    for n in range(len(PROMPT_IN)):
+    def prompt_in(n):
         others(nm, m, lambda p: copy_b(n, m, p).start())
+
+    prompt_in(0)
 
     load_q.wait()
     load_d.wait()
@@ -206,24 +214,38 @@
             send_sem=p_send.at[n, owner], recv_sem=p_recv.at[n, src],
             device_id={"resp": resp_of(owner)}, device_id_type=MESH)
 
-    def store_out(g, which):
-        cols = pl.ds(pl.multiple_of(g * ROWS, ROWS), ROWS)
-        src, dst = ((ov, out_hbm), (dqv, dq_hbm))[which]
-        return pltpu.make_async_copy(src.at[:, cols], dst.at[:, cols], out_sem.at[which, g])
+    def sum_prompt(n):
+        g0, count = PROMPT_OUT[n]
+        heads = pl.ds(g0, count)
+        others(nm, m, lambda p: copy_p(n, m, p).wait_recv())
+        for h in range(2):
+            psum[h, heads] = term[heads, :, pair_rows(m, h, 1), :].astype(F32)
+
+        def add(p):
+            for h in range(2):
+                psum[h, heads] += pterm[p, heads, :, h * prow:(h + 1) * prow, :].astype(F32)
+
+        others(nm, m, add)
 
     def head(g):
         for n, (g0, _) in enumerate(PROMPT_IN):
             @pl.when(g == g0)
             def _():
                 others(nm, m, lambda p: copy_b(n, p, p).wait_recv())
+        for n in (1, 2):
+            @pl.when(g == n - 1)
+            def _():
+                prompt_in(n)
+
         for n, (g0, _) in enumerate(GATHER):
             @pl.when(g == g0)
             def _():
                 loop(0, c, lambda j: copy_g(n, j, j).wait_recv())
-            if n >= 3:
-                @pl.when(g == g0 - 4)
-                def _():
-                    gather(n)
+
+        for n in range(1, KVH):
+            @pl.when((g == n - 2) & (n >= 2))
+            def _():
+                gather(n)
 
         cols = [pl.ds(pl.multiple_of(g * ROWS + a * HD, HD), HD) for a in range(G)]
         k = kv[g, 0]
@@ -232,25 +254,20 @@
         d = jnp.concatenate([jnp.where(live, dv[:, x], jnp.zeros((), BF)) for x in cols], 0)
         limit = jnp.concatenate([causal_cols[...]] * G, 0)
         s = dot_nt(jnp.concatenate([k, hidden_cols[...]], 1), jnp.concatenate([q, limit], 1))
+        dp = dot_nt(v, d)
         top = jnp.max(s, 0, keepdims=True)
         p = jnp.exp2((s - top) * (SCALE * LOG2E))
         inv = 1.0 / jnp.sum(p, 0, keepdims=True)
         p = p.astype(BF)
-        out = dot(v.T, p) * (inv * jnp.concatenate([live_lane] * G, 1))
-        out = out.T.astype(BF)
+        out = (dot(v.T, p) * (inv * jnp.concatenate([live_lane] * G, 1))).astype(BF)
+        corr = jnp.sum(d.T.astype(F32) * out.astype(F32), 0, keepdims=True)
+        out = out.T
         for a in range(G):
             ov[:, cols[a]] = out[a * TOK:(a + 1) * TOK]
-        store_out(g, 0).start()
-        corr = -jnp.sum(d.astype(F32) * out.astype(F32), 1, keepdims=True)
-        high = corr.astype(BF).astype(F32)
-        lane = iota((ROWS, HD), 1)
-        corr_cols = jnp.where(lane == 0, high, jnp.where(lane == 1, corr - high, 0.0)).astype(BF)
-        dp = dot_nt(jnp.concatenate([v, ones_cols[...]], 1), jnp.concatenate([d, corr_cols], 1))
-        ds = (p.astype(F32) * dp).astype(BF)
+        ds = p * (dp - corr).astype(BF)
         dq = (dot(k.T, ds) * (inv * SCALE)).T.astype(BF)
         for a in range(G):
             dqv[:, cols[a]] = dq[a * TOK:(a + 1) * TOK]
-        store_out(g, 1).start()
         inv_col = jnp.broadcast_to(inv, (HD, ROWS)).T
         term[g, 1] = dot(p, (d.astype(F32) * inv_col).astype(BF)).astype(BF)
         term[g, 0] = dot(ds, (q.astype(F32) * (inv_col * SCALE)).astype(BF)).astype(BF)
@@ -263,18 +280,14 @@
             def _():
                 others(nm, m, lambda p: copy_p(n, p, m).start())
 
+        @pl.when(g == 6)
+        def _():
+            sum_prompt(0)
+
     loop(0, KVH, head)
 
-    for n in range(len(PROMPT_OUT)):
-        others(nm, m, lambda p: copy_p(n, m, p).wait_recv())
-    for h in range(2):
-        psum[h] = term[:, :, pair_rows(m, h, 1), :].astype(F32)
-
-    def add_p(p):
-        for h in range(2):
-            psum[h] += pterm[p, :, :, h * prow:(h + 1) * prow, :].astype(F32)
-
-    others(nm, m, add_p)
+    sum_prompt(1)
+    sum_prompt(2)
     xsend[...] = psum[1 - half].astype(BF)
     swap_back = copy_x(1, xsend, xrecv)
     swap_back.start()
@@ -324,12 +337,6 @@
     for n in range(len(TERMS)):
         loop(0, c, lambda j: copy_t(n, j, c).wait_send())
 
-    def finish(g):
-        store_out(g, 0).wait()
-        store_out(g, 1).wait()
-
-    loop(0, KVH, finish)
-
 
 def per_device(
     nr, nc, queries, resp_keys, resp_values, prompt_keys, prompt_values, upstream, lengths, prompt_length
@@ -339,7 +346,7 @@
     width = KVH * HD
     vmem = pl.BlockSpec(memory_space=pltpu.VMEM)
     smem = pl.BlockSpec(memory_space=pltpu.SMEM)
-    hbm = pl.BlockSpec(memory_space=pl.ANY)
+    hbm = pl.BlockSpec(memory_space=pltpu.HBM)
     dma = pltpu.SemaphoreType.DMA
     big = jax.ShapeDtypeStruct((TOK, KVH * ROWS), BF)
     grad = jax.ShapeDtypeStruct((TOK, width), F32)
@@ -347,17 +354,18 @@
     outs = pl.pallas_call(
         functools.partial(kernel, nr, nc),
         out_shape=(big, big, grad, grad, small, small),
-        in_specs=[hbm, hbm, vmem, vmem, vmem, vmem, smem, smem],
-        out_specs=[hbm, hbm, vmem, vmem, vmem, vmem],
+        in_specs=[hbm] * 6 + [smem, smem],
+        out_specs=[vmem] * 6,
         scratch_shapes=[
             pltpu.VMEM((TOK, KVH * ROWS), BF),
             pltpu.VMEM((TOK, KVH * ROWS), BF),
-            pltpu.VMEM((TOK, KVH * ROWS), BF),
-            pltpu.VMEM((TOK, KVH * ROWS), BF),
+            pltpu.VMEM((TOK, width), BF),
+            pltpu.VMEM((TOK, width), BF),
+            pltpu.VMEM((2, width), BF),
+            pltpu.VMEM((2, width), BF),
             pltpu.VMEM((KVH, 2, key_rows, HD), BF),
             pltpu.VMEM((KVH, 2, key_rows, HD), BF),
             pltpu.VMEM((nc, KVH, 2, TOK, HD), BF),
-            pltpu.VMEM((key_rows, HD), BF),
             pltpu.VMEM((key_rows, HD), BF),
             pltpu.VMEM((TOK, HD), BF),
             pltpu.VMEM((2, nc, 2, 16, HD), BF),
@@ -367,7 +375,7 @@
             pltpu.VMEM((KVH, 2, prow, HD), BF),
             pltpu.VMEM((KVH, 2, prow, HD), BF),
             pltpu.VMEM((nc, 2, 16, HD), BF),
-            dma((2,)), dma((2, KVH)), dma((2, 2)),
+            dma((6,)), dma((2, 2)),
             dma((nc,)), dma((nc,)),
             dma((len(PROMPT_IN), nr // 2)), dma((len(PROMPT_IN), nr // 2)),
             dma((len(GATHER), nc)), dma((len(GATHER), nc)),
@@ -376,7 +384,7 @@
             dma((nc,)), dma((nc,)),
         ],
         compiler_params=pltpu.CompilerParams(
-            collective_id=0, has_side_effects=True, vmem_limit_bytes=60 * 2**20),
+            collective_id=0, has_side_effects=True, vmem_limit_bytes=58 * 2**20),
         cost_estimate=pl.CostEstimate(
             flops=12 * KVH * ROWS * key_rows * HD, bytes_accessed=10 * 2**20,
             transcendentals=KVH * ROWS * key_rows),

time: 105 us -> 94.3 us (0.90); the launches traced: 103 us -> 94.2 us
  Pallas kernels: 94.1 us -> 84.8 us
    pallas_call x1, Pallas kernels: 94.1 us -> 84.8 us  [per_device(): pl.pallas_call(functools.partial(kernel, nr, nc), out_shape=(big, big, gr...]
where the time goes in v3:
time: 94.3 us; the launch traced here: 94.2 us
  Pallas kernels  84.8 us (90%)
  local copies, waits for them, and re-layouts  7.41 us (8%)
  between operations  1.95 us (2%)
    pallas_call x1, Pallas kernels, per_device(): pl.pallas_call(functools.partial(kernel, nr, nc), out_shape=(big, big, gr...  84.8 us
    unnamed x16, local copies, waits for them, and re-layouts  7.41 us

profile of v3, /device:TPU:0, one launch (start us, length us, event | category | flops | bytes accessed | tf_op | source)
XLA Modules:
  0.0 94.2 jit_solution(2425902923909435154)
XLA Ops:
  1.9 84.8 %shard_map.127 = (bf16[128,8192]{1,0:T(8,128)(2,1)}, bf16[128,8192]{1,0:T(8,128)(2,1)}, f32[128,1024]{1,0:T(8,128)}, f32[128,1024]{1,0:T(8,128)}, f32[2,1024]{1,0:T(2,128)}, /*index=5*/f32[2,1024]{1,0:T(2,128)}) custom-call(bf16[128,8192]{1,0:T(8,128)(2,1)} %bitcast.12, bf16[128,8192]{1,0:T(8,128)(2,1)} %bitcast.13, bf16[128,1024]{1,0:T(8,128)(2,1)} %bitcast.14, ...), custom_call_target="tpu_custom_call" | custom-call | flops 16106127360 | bytes 10485760 | tf_op jit(solution)/shard_map/pallas_call | solution.py:354
  86.7 0.0 copy-start
  86.7 3.2 %copy.22 = bf16[1,128,8192]{2,1,0:T(8,128)(2,1)} copy(bf16[1,128,8192]{2,1,0:T(8,128)(2,1)} %bitcast.9) | data formatting | bytes 4194304
  90.0 0.0 copy-done
  90.0 0.0 copy-start.2
  90.0 0.0 copy-start.1
  90.0 1.3 %copy.23 = bf16[1,128,8192]{2,1,0:T(8,128)(2,1)} copy(bf16[1,128,8192]{2,1,0:T(8,128)(2,1)S(1)} %bitcast.8) | data formatting | bytes 4194304
  91.3 0.1 copy-done.2
  91.4 0.0 copy-start.4
  91.4 0.0 copy-start.3
  91.4 0.8 copy.24
  92.2 0.0 copy-done.1
  92.2 0.8 copy.25
  93.0 0.0 copy-done.4
  93.0 0.6 copy.26
  93.6 0.0 copy-done.3
  93.6 0.6 copy.27
Async XLA Ops:
  86.7 3.3 %copy-start = (bf16[128,8192]{1,0:T(8,128)(2,1)S(1)}, bf16[128,8192]{1,0:T(8,128)(2,1)}, u32[]{:S(2)}) copy-start(bf16[128,8192]{1,0:T(8,128)(2,1)} %get-tuple-element.13) | copy-start | bytes 6291460
  90.0 1.4 %copy-start.2 = (f32[128,1024]{1,0:T(8,128)S(1)}, f32[128,1024]{1,0:T(8,128)}, u32[]{:S(2)}) copy-start(f32[128,1024]{1,0:T(8,128)} %get-tuple-element.14) | copy-start | bytes 1572868
  90.0 2.2 %copy-start.1 = (f32[128,1024]{1,0:T(8,128)S(1)}, f32[128,1024]{1,0:T(8,128)}, u32[]{:S(2)}) copy-start(f32[128,1024]{1,0:T(8,128)} %get-tuple-element.15) | copy-start | bytes 1572868
  91.4 1.6 %copy-start.4 = (f32[2,1024]{1,0:T(2,128)S(1)}, f32[2,1024]{1,0:T(2,128)}, u32[]{:S(2)}) copy-start(f32[2,1024]{1,0:T(2,128)} %get-tuple-element.28) | copy-start | bytes 24580
  91.4 2.2 %copy-start.3 = (f32[2,1024]{1,0:T(2,128)S(1)}, f32[2,1024]{1,0:T(2,128)}, u32[]{:S(2)}) copy-start(f32[2,1024]{1,0:T(2,128)} %get-tuple-element.29) | copy-start | bytes 24580

commit v4 on v3

--- a/solution.py
+++ b/solution.py
@@ -22,8 +22,6 @@
 
 PROMPT_IN = ((0, 1), (1, 2), (3, 5))
 PROMPT_OUT = ((0, 4), (4, 3), (7, 1))
-GATHER = tuple((g, 1) for g in range(8))
-TERMS = tuple((g, 1) for g in range(8))
 
 
 def iota(shape, axis):
@@ -110,8 +108,7 @@
     others(nc, c, lambda p: copy_a(c, p).start())
 
     def copy_g(n, slot, peer):
-        g0, count = GATHER[n]
-        part = kv.at[pl.ds(g0, count), :, block_rows(slot), :]
+        part = kv.at[n, :, block_rows(slot), :]
         return pltpu.make_async_remote_copy(
             src_ref=part, dst_ref=part,
             send_sem=g_send.at[n, peer], recv_sem=g_recv.at[n, slot],
@@ -198,12 +195,10 @@
     load_q.wait()
     load_d.wait()
 
-    def copy_t(n, block, src):
-        g0, count = TERMS[n]
-        return pltpu.make_async_remote_copy(
-            src_ref=term.at[pl.ds(g0, count), :, block_rows(block), :],
-            dst_ref=rterm.at[src, pl.ds(g0, count)],
-            send_sem=t_send.at[n, block], recv_sem=t_recv.at[n, src],
+    def copy_t(g, block, src):
+        return pltpu.make_async_remote_copy(
+            src_ref=term.at[g, :, block_rows(block), :], dst_ref=rterm.at[src, g],
+            send_sem=t_send.at[g, block], recv_sem=t_recv.at[g, src],
             device_id={"ctx": block}, device_id_type=MESH)
 
     def copy_p(n, owner, src):
@@ -237,15 +232,11 @@
             def _():
                 prompt_in(n)
 
-        for n, (g0, _) in enumerate(GATHER):
-            @pl.when(g == g0)
-            def _():
-                loop(0, c, lambda j: copy_g(n, j, j).wait_recv())
-
-        for n in range(1, KVH):
-            @pl.when((g == n - 2) & (n >= 2))
-            def _():
-                gather(n)
+        @pl.when(g + 2 < KVH)
+        def _():
+            gather(g + 2)
+
+        loop(0, c, lambda j: copy_g(g, j, j).wait_recv())
 
         cols = [pl.ds(pl.multiple_of(g * ROWS + a * HD, HD), HD) for a in range(G)]
         k = kv[g, 0]
@@ -265,16 +256,13 @@
         for a in range(G):
             ov[:, cols[a]] = out[a * TOK:(a + 1) * TOK]
         ds = p * (dp - corr).astype(BF)
+        inv_col = jnp.broadcast_to(inv, (HD, ROWS)).T
+        term[g, 1] = dot(p, (d.astype(F32) * inv_col).astype(BF)).astype(BF)
+        term[g, 0] = dot(ds, (q.astype(F32) * (inv_col * SCALE)).astype(BF)).astype(BF)
+        loop(0, c, lambda j: copy_t(g, j, c).start())
         dq = (dot(k.T, ds) * (inv * SCALE)).T.astype(BF)
         for a in range(G):
             dqv[:, cols[a]] = dq[a * TOK:(a + 1) * TOK]
-        inv_col = jnp.broadcast_to(inv, (HD, ROWS)).T
-        term[g, 1] = dot(p, (d.astype(F32) * inv_col).astype(BF)).astype(BF)
-        term[g, 0] = dot(ds, (q.astype(F32) * (inv_col * SCALE)).astype(BF)).astype(BF)
-        for n, (g0, count) in enumerate(TERMS):
-            @pl.when(g == g0 + count - 1)
-            def _():
-                loop(0, c, lambda j: copy_t(n, j, c).start())
         for n, (g0, count) in enumerate(PROMPT_OUT):
             @pl.when(g == g0 + count - 1)
             def _():
@@ -308,13 +296,12 @@
 
     others(nc, c, lambda p: copy_z(p, c).start())
 
-    for n, (g0, count) in enumerate(TERMS):
-        loop(c + 1, nc, lambda src: copy_t(n, c, src).wait_recv())
-        for g in range(g0, g0 + count):
-            for w, ref in enumerate((kg_ref, vg_ref)):
-                ref[:, g * HD:(g + 1) * HD] = lax.fori_loop(
-                    c + 1, nc, lambda src, total: total + rterm[src, g, w].astype(F32),
-                    term[g, w, block_rows(c), :].astype(F32))
+    for g in range(KVH):
+        loop(c + 1, nc, lambda src: copy_t(g, c, src).wait_recv())
+        for w, ref in enumerate((kg_ref, vg_ref)):
+            ref[:, g * HD:(g + 1) * HD] = lax.fori_loop(
+                c + 1, nc, lambda src, total: total + rterm[src, g, w].astype(F32),
+                term[g, w, block_rows(c), :].astype(F32))
 
     others(nc, c, lambda p: copy_z(c, p).wait_recv())
     for w, ref in enumerate((pkg_ref, pvg_ref)):
@@ -332,10 +319,11 @@
     for n in range(len(PROMPT_OUT)):
         others(nm, m, lambda p: copy_p(n, p, m).wait_send())
     others(nc, c, lambda p: copy_z(p, c).wait_send())
-    for n in range(len(GATHER)):
-        loop(c + 1, nc, lambda p: copy_g(n, c, p).wait_send())
-    for n in range(len(TERMS)):
-        loop(0, c, lambda j: copy_t(n, j, c).wait_send())
+    def finish(g):
+        loop(c + 1, nc, lambda p: copy_g(g, c, p).wait_send())
+        loop(0, c, lambda j: copy_t(g, j, c).wait_send())
+
+    loop(0, KVH, finish)
 
 
 def per_device(
@@ -378,8 +366,8 @@
             dma((6,)), dma((2, 2)),
             dma((nc,)), dma((nc,)),
             dma((len(PROMPT_IN), nr // 2)), dma((len(PROMPT_IN), nr // 2)),
-            dma((len(GATHER), nc)), dma((len(GATHER), nc)),
-            dma((len(TERMS), nc)), dma((len(TERMS), nc)),
+            dma((KVH, nc)), dma((KVH, nc)),
+            dma((KVH, nc)), dma((KVH, nc)),
             dma((len(PROMPT_OUT), nr // 2)), dma((len(PROMPT_OUT), nr // 2)),
             dma((nc,)), dma((nc,)),
         ],

time: 94.3 us -> 94.7 us (level)
  no operation moved by 1% of the time
where the time goes in v4:
time: 94.7 us; the launch traced here: 94.6 us
  Pallas kernels  85.2 us (90%)
  local copies, waits for them, and re-layouts  7.41 us (8%)
  between operations  1.95 us (2%)
    pallas_call x1, Pallas kernels, per_device(): pl.pallas_call(functools.partial(kernel, nr, nc), out_shape=(big, big, gr...  85.2 us
    unnamed x16, local copies, waits for them, and re-layouts  7.41 us

profile of v4, /device:TPU:0, one launch (start us, length us, event | category | flops | bytes accessed | tf_op | source)
XLA Modules:
  0.0 94.6 jit_solution(4304204814618794764)
XLA Ops:
  1.9 85.2 %shard_map.127 = (bf16[128,8192]{1,0:T(8,128)(2,1)}, bf16[128,8192]{1,0:T(8,128)(2,1)}, f32[128,1024]{1,0:T(8,128)}, f32[128,1024]{1,0:T(8,128)}, f32[2,1024]{1,0:T(2,128)}, /*index=5*/f32[2,1024]{1,0:T(2,128)}) custom-call(bf16[128,8192]{1,0:T(8,128)(2,1)} %bitcast.12, bf16[128,8192]{1,0:T(8,128)(2,1)} %bitcast.13, bf16[128,1024]{1,0:T(8,128)(2,1)} %bitcast.14, ...), custom_call_target="tpu_custom_call" | custom-call | flops 16106127360 | bytes 10485760 | tf_op jit(solution)/shard_map/pallas_call | solution.py:342
  87.1 0.0 copy-start
  87.2 3.2 %copy.22 = bf16[1,128,8192]{2,1,0:T(8,128)(2,1)} copy(bf16[1,128,8192]{2,1,0:T(8,128)(2,1)} %bitcast.9) | data formatting | bytes 4194304
  90.4 0.0 copy-done
  90.4 0.0 copy-start.2
  90.4 0.0 copy-start.1
  90.4 1.3 %copy.23 = bf16[1,128,8192]{2,1,0:T(8,128)(2,1)} copy(bf16[1,128,8192]{2,1,0:T(8,128)(2,1)S(1)} %bitcast.8) | data formatting | bytes 4194304
  91.7 0.1 copy-done.2
  91.8 0.0 copy-start.4
  91.8 0.0 copy-start.3
  91.8 0.8 copy.24
  92.6 0.0 copy-done.1
  92.6 0.8 copy.25
  93.4 0.0 copy-done.4
  93.4 0.6 copy.26
  94.0 0.0 copy-done.3
  94.0 0.6 copy.27
Async XLA Ops:
  87.1 3.3 %copy-start = (bf16[128,8192]{1,0:T(8,128)(2,1)S(1)}, bf16[128,8192]{1,0:T(8,128)(2,1)}, u32[]{:S(2)}) copy-start(bf16[128,8192]{1,0:T(8,128)(2,1)} %get-tuple-element.13) | copy-start | bytes 6291460
  90.4 1.4 %copy-start.2 = (f32[128,1024]{1,0:T(8,128)S(1)}, f32[128,1024]{1,0:T(8,128)}, u32[]{:S(2)}) copy-start(f32[128,1024]{1,0:T(8,128)} %get-tuple-element.14) | copy-start | bytes 1572868
  90.4 2.2 %copy-start.1 = (f32[128,1024]{1,0:T(8,128)S(1)}, f32[128,1024]{1,0:T(8,128)}, u32[]{:S(2)}) copy-start(f32[128,1024]{1,0:T(8,128)} %get-tuple-element.15) | copy-start | bytes 1572868
  91.8 1.6 %copy-start.4 = (f32[2,1024]{1,0:T(2,128)S(1)}, f32[2,1024]{1,0:T(2,128)}, u32[]{:S(2)}) copy-start(f32[2,1024]{1,0:T(2,128)} %get-tuple-element.28) | copy-start | bytes 24580
  91.8 2.2 %copy-start.3 = (f32[2,1024]{1,0:T(2,128)S(1)}, f32[2,1024]{1,0:T(2,128)}, u32[]{:S(2)}) copy-start(f32[2,1024]{1,0:T(2,128)} %get-tuple-element.29) | copy-start | bytes 24580
